TPU v7x, 32 devices: a whole 2x2x4 slice. The times are simulated.
32 devices in a mesh: groups: 2 (over x), ent: 16 (over z, y, core).
Axes of the slice: x: 2, y: 2, z: 4, core: 2. Of those that a mesh axis runs over, the one named last changes fastest.
Arguments:
- entity: float32 [32768, 400], P(('groups', 'ent')), parts along dimension 0, may hold values from -4 to 4
- entity_state: float32 [32768], P(('groups', 'ent')), parts along dimension 0, may hold values from 0.01 to 1
- relation: float32 [4352, 400], P('groups'), parts along dimension 0, may hold values from 0.5 to 1.5
- relation_state: float32 [4352], P('groups'), parts along dimension 0, may hold values from 0.01 to 1
- src_offset: int32 [32768], P(('groups', 'ent')), parts along dimension 0, may hold values from 0 to 1023
- dst_part: int32 [32768, 1], P(('groups', 'ent')), parts along dimension 0, may hold values from 0 to 15; in each aligned block of 1024 rows (0 to 1023, 1024 to 2047, ...) at most 128 rows name the same one
- dst_offset: int32 [32768], P(('groups', 'ent')), parts along dimension 0, may hold values from 0 to 1023
- rel_id: int32 [32768], P(('groups', 'ent')), parts along dimension 0, may hold values from 0 to 2175
Outputs:
- new_entity: float32 [32768, 400], P(('groups', 'ent')), parts along dimension 0
- new_entity_state: float32 [32768], P(('groups', 'ent')), parts along dimension 0
- new_relation: float32 [4352, 400], P('groups'), parts along dimension 0
- new_relation_state: float32 [4352], P('groups'), parts along dimension 0
- edge_loss: float32 [32768], P(('groups', 'ent')), parts along dimension 0
There are 2 independent parts, one for each index of `groups`. A program takes and returns all parts, laid end to end along the dimension named above; each array names one. Nothing has to cross between parts.
Inputs may be any that keep to these rules, and one draw needn't show every extreme that they name: `dst_part`: at most 128 of the edges held by one partition have one destination partition, and in every draw some partition has exactly 128 edges for one destination partition.
All inputs are finite; a program needn't handle non-finite values.
Results may differ from a plain program's by a relative error of at most 0.0024.
Values may be sent and summed in bfloat16 or wider, within the bound.
A program may use at most 128 MiB of HBM per device.

v0:
```python
import jax
import jax.numpy as jnp
from jax import lax
from jax.sharding import PartitionSpec as P

BLOCK = 1024


learn_rate = 0.3


def score_one(pair):
    query_block, target_block = pair
    block_rows = query_block.shape[0]
    logits = jnp.dot(query_block, target_block.T, preferred_element_type=jnp.float32)
    row_max = jnp.max(logits, axis=1, keepdims=True)
    shifted = jnp.exp(logits - row_max)
    total = jnp.sum(shifted, axis=1, keepdims=True)
    log_total = jnp.log(total) + row_max
    on_diag = lax.broadcasted_iota(jnp.int32, (block_rows, block_rows), 0) == lax.broadcasted_iota(
        jnp.int32, (block_rows, block_rows), 1
    )
    positive = jnp.sum(jnp.where(on_diag, logits, 0.0), axis=1)
    edge_loss = log_total[:, 0] - positive
    softmax_w = jnp.exp(logits - log_total)
    coefficient = jnp.where(on_diag, softmax_w - 1.0, softmax_w).astype(jnp.bfloat16)
    query_grad = jnp.dot(coefficient, target_block, preferred_element_type=jnp.float32)
    target_grad = lax.dot_general(
        coefficient, query_block, (((0,), (0,)), ((), ())), preferred_element_type=jnp.float32
    )
    return (edge_loss, query_grad, target_grad)


def on_device(
    entity, entity_state, relation, relation_state, src_offset, dst_part, dst_offset, rel_id
):
    row_count, feat_dim = entity.shape
    edge_count = src_offset.shape[0]
    owners = lax.axis_size("ent")
    capacity = max(2, 2 * edge_count // owners)
    dest_part = dst_part[:, 0]
    onehot = (dest_part[:, None] == jnp.arange(owners, dtype=jnp.int32)[None, :]).astype(jnp.int32)
    before = jnp.cumsum(onehot, axis=0) - onehot
    slot_rank = jnp.sum(before * onehot, axis=1)
    slot_index = dest_part * capacity + slot_rank
    requests = jnp.zeros((owners * capacity,), jnp.int32).at[slot_index].set(dst_offset)
    requests = requests.reshape(owners, capacity)
    offsets = lax.all_to_all(requests, "ent", split_axis=0, concat_axis=0, tiled=True)
    looked = entity[offsets].astype(jnp.bfloat16)
    replies = lax.all_to_all(looked, "ent", split_axis=0, concat_axis=0, tiled=True)
    targets = replies.reshape(owners * capacity, feat_dim)[slot_index]
    sources = entity[src_offset]
    weights = relation[rel_id]
    queries = (sources * weights).astype(jnp.bfloat16)
    block_count = edge_count // BLOCK
    edge_loss, query_grad, target_grad = lax.map(
        score_one,
        (
            queries.reshape(block_count, BLOCK, feat_dim),
            targets.reshape(block_count, BLOCK, feat_dim),
        ),
    )
    edge_loss = edge_loss.reshape(edge_count)
    query_grad = query_grad.reshape(edge_count, feat_dim)
    target_grad = target_grad.reshape(edge_count, feat_dim)
    returned = jnp.zeros((owners * capacity, feat_dim), jnp.float32).at[slot_index].set(target_grad)
    returned = returned.reshape(owners, capacity, feat_dim)
    arrived = lax.all_to_all(returned, "ent", split_axis=0, concat_axis=0, tiled=True)
    entity_grad = (
        jnp.zeros((row_count, feat_dim), jnp.float32).at[src_offset].add(query_grad * weights)
    )
    entity_grad = entity_grad.at[offsets.reshape(owners * capacity)].add(
        arrived.reshape(owners * capacity, feat_dim)
    )
    state_next = entity_state + jnp.mean(entity_grad * entity_grad, axis=1)
    new_entity = entity - learn_rate * entity_grad / jnp.sqrt(state_next)[:, None]
    relation_terms = jnp.zeros(relation.shape, jnp.float32).at[rel_id].add(query_grad * sources)
    relation_grad = lax.psum(relation_terms, "ent")
    relation_next = relation_state + jnp.mean(relation_grad * relation_grad, axis=1)
    new_relation = relation - learn_rate * relation_grad / jnp.sqrt(relation_next)[:, None]
    return (new_entity, state_next, new_relation, relation_next, edge_loss)


def solution(mesh):
    placed = (
        P(("groups", "ent"), None),
        P(("groups", "ent")),
        P("groups", None),
        P("groups"),
        P(("groups", "ent")),
        P(("groups", "ent"), None),
        P(("groups", "ent")),
        P(("groups", "ent")),
    )
    return jax.shard_map(
        on_device,
        mesh=mesh,
        in_specs=placed,
        out_specs=(
            P(("groups", "ent"), None),
            P(("groups", "ent")),
            P("groups", None),
            P("groups"),
            P(("groups", "ent")),
        ),
        check_vma=False,
    )
```

profile of v0, /device:TPU:0, one launch (start us, length us, event | category | flops | bytes accessed | tf_op | source)
XLA Modules:
  0.0 343.8 jit_solution(7144858125063748535)
XLA Ops:
  7.9 4.5 %reduce-window.6 = s32[16,8,128]{2,1,0:T(8,128)S(1)} reduce-window(s32[16,8,128]{2,1,0:T(8,128)S(1)} %fusion.10, s32[]{:T(128)} %constant.17.clone.1), window={size=1x1x128 pad=0_0x0_0x127_0}, to_apply=%region_0.0 | reduce-window | flops 2080768 | bytes 131076 | tf_op jit(solution)/shard_map/reduce-window
  14.2 5.0 %scatter_custom_fusion = s32[2048]{0:T(1024)} fusion(s32[1024]{0:T(1024)S(1)} %bitcast.52, s32[1024]{0:T(1024)} %param.14, s32[]{:T(128)} %constant.17.clone.1), kind=kCustom, calls=%fused_computation.43 | custom fusion | bytes 8704 | tf_op jit(solution)/shard_map/scatter | solution.py:46
  19.2 7.4 %all-to-all-start = ((s32[16,1,128]{2,1,0:T(1,128)}), s32[16,1,128]{2,1,0:T(1,128)S(1)}, u32[]{:S(2)}, u32[]{:S(2)}) async-start(s32[16,1,128]{2,1,0:T(1,128)} %bitcast.6), calls=%async_computation | async-start | bytes 16384 | tf_op jit(solution)/shard_map/all_to_all | solution.py:48
  26.6 1.8 copy.64
  28.5 4.5 %all-to-all-done = s32[16,1,128]{2,1,0:T(1,128)S(1)} async-done(((s32[16,1,128]{2,1,0:T(1,128)}), s32[16,1,128]{2,1,0:T(1,128)S(1)}, u32[]{:S(2)}, u32[]{:S(2)}) %all-to-all-start) | async-done | bytes 8224 | tf_op jit(solution)/shard_map/all_to_all | solution.py:48
  33.0 8.6 %gather_fusion.2 = bf16[2048,400]{1,0:T(8,128)(2,1)} fusion(f32[1024,400]{1,0:T(8,128)S(1)} %copy.64, s32[2048]{0:T(1024)S(1)} %fusion.12), kind=kCustom, calls=%fused_computation.2 | custom fusion | bytes 3284992 | tf_op jit(solution)/shard_map/gather | solution.py:49
  41.6 3.9 %copy.56 = bf16[16,128,400]{1,2,0:T(8,128)(2,1)} copy(bf16[16,128,400]{2,1,0:T(8,128)(2,1)} %bitcast.44) | data formatting | bytes 3276800 | tf_op jit(solution)/shard_map/convert_element_type | solution.py:49
  45.5 4.5 %all-to-all-start.1 = ((bf16[16,128,400]{1,2,0:T(8,128)(2,1)}), bf16[16,128,400]{1,2,0:T(8,128)(2,1)}, u32[]{:S(2)}, u32[]{:S(2)}) async-start(bf16[16,128,400]{1,2,0:T(8,128)(2,1)} %copy.56), calls=%async_computation.1 | async-start | bytes 3276800 | tf_op jit(solution)/shard_map/all_to_all | solution.py:50
  50.1 4.9 %gather_fusion = f32[1024,400]{1,0:T(8,128)} fusion(f32[1024,400]{1,0:T(8,128)S(1)} %copy.64, s32[1024]{0:T(1024)S(1)} %get-tuple-element.50), kind=kCustom, calls=%fused_computation | custom fusion | bytes 3280896 | tf_op jit(solution)/shard_map/gather | solution.py:52
  54.9 5.3 %copy.52 = f32[2176,400]{1,0:T(8,128)} copy(f32[2176,400]{0,1:T(8,128)} %param.10) | data formatting | bytes 6963200 | tf_op args[2]
  60.3 7.7 %gather_fusion.1 = f32[1024,400]{1,0:T(8,128)} fusion(f32[2176,400]{1,0:T(8,128)} %copy.52, s32[1024]{0:T(1024)S(1)} %get-tuple-element.49), kind=kCustom, calls=%fused_computation.1 | custom fusion | bytes 3280896 | tf_op jit(solution)/shard_map/gather | solution.py:53
  68.0 3.0 multiply_convert_fusion
  71.0 12.2 %all-to-all-done.1 = bf16[16,128,400]{1,2,0:T(8,128)(2,1)} async-done(((bf16[16,128,400]{1,2,0:T(8,128)(2,1)}), bf16[16,128,400]{1,2,0:T(8,128)(2,1)}, u32[]{:S(2)}, u32[]{:S(2)}) %all-to-all-start.1) | async-done | bytes 1638432 | tf_op jit(solution)/shard_map/all_to_all | solution.py:50
  83.1 2.8 copy.57
  85.9 4.0 %gather_fusion.3 = bf16[1024,400]{1,0:T(8,128)(2,1)S(1)} fusion(bf16[2048,400]{1,0:T(8,128)(2,1)S(1)} %bitcast.41, s32[1024]{0:T(1024)S(1)} %broadcast_clamp_fusion), kind=kCustom, calls=%fused_computation.3 | custom fusion | bytes 1642496 | tf_op jit(solution)/shard_map/gather | solution.py:51
  89.9 2.5 fusion.23
  95.7 7.0 %scatter_custom_fusion.2 = f32[2048,400]{1,0:T(8,128)} fusion(s32[1024]{0:T(1024)S(1)} %bitcast.54, f32[1024,400]{1,0:T(8,128)S(1)} %fusion.15, f32[]{:T(128)} %constant.16.clone.1), kind=kCustom, calls=%fused_computation.20 | custom fusion | bytes 3276804 | tf_op jit(solution)/shard_map/scatter | solution.py:66
  102.7 5.3 %copy.61 = f32[16,128,400]{1,2,0:T(8,128)} copy(f32[16,128,400]{2,1,0:T(8,128)} %bitcast.43) | data formatting | bytes 6553600 | tf_op jit(solution)/shard_map/reshape | solution.py:67
  107.9 9.5 %all-to-all-start.2 = ((f32[16,128,400]{1,2,0:T(8,128)}), f32[16,128,400]{1,2,0:T(8,128)}, u32[]{:S(2)}, u32[]{:S(2)}) async-start(f32[16,128,400]{1,2,0:T(8,128)} %copy.61), calls=%async_computation.2 | async-start | bytes 6553600 | tf_op jit(solution)/shard_map/all_to_all | solution.py:68
  119.4 2.7 copy.58
  122.1 5.4 %fusion.22 = (f32[1024,400]{0,1:T(8,128)}, f32[1024,400]{0,1:T(8,128)S(1)}) fusion(f32[1024,400]{0,1:T(8,128)} %copy.65, f32[1024,400]{0,1:T(8,128)} %copy.58, bf16[1024,400]{1,0:T(8,128)(2,1)S(1)} %gather_fusion.3, f32[1024,1024]{0,1:T(8,128)} %copy-done.2, f32[1024]{0:T(1024)S(1)} %get-tuple-element.41), kind=kOutput, calls=%fused_computation.53 | convolution fusion | flops 844922880 | bytes 11571200 | tf_op jit(solution)/shard_map/while/body/eval_jaxpr/dot_general | solution.py:27
  127.5 2.8 copy.66
  130.3 9.6 %scatter_custom_fusion.4 = f32[2176,400]{1,0:T(8,128)} fusion(s32[1024]{0:T(1024)S(1)} %get-tuple-element.48, f32[1024,400]{1,0:T(8,128)} %copy.66, f32[]{:T(128)} %constant.16.clone.1), kind=kCustom, calls=%fused_computation.16 | custom fusion | flops 409600 | bytes 3482112 | tf_op jit(solution)/shard_map/scatter-add | solution.py:77
  139.9 1.8 copy.59
  141.7 7.8 %scatter_custom_fusion.1 = f32[1024,400]{1,0:T(8,128)S(1)} fusion(s32[1024]{0:T(1024)S(1)} %get-tuple-element.51, f32[1024,400]{1,0:T(8,128)} %copy.59, f32[]{:T(128)} %constant.16.clone.1), kind=kCustom, calls=%fused_computation.23 | custom fusion | flops 409600 | bytes 1638912 | tf_op jit(solution)/shard_map/scatter-add | solution.py:70
  149.5 146.8 %all-reduce.2.cloned.1.call-done = f32[2176,400]{1,0:T(8,128)} async-done(((f32[2176,400]{1,0:T(8,128)}), f32[2176,400]{1,0:T(8,128)}) %all-reduce.2.cloned.1.call-update) | async-done | bytes 3481616 | tf_op jit(solution)/shard_map/psum | solution.py:78
  296.3 2.8 multiply_reduce_fusion
  299.9 5.1 %divide_subtract_fusion = f32[2176,400]{1,0:T(8,128)} fusion(f32[2176,400]{1,0:T(8,128)} %copy.52, f32[2176,400]{1,0:T(8,128)S(1)} %copy-done.5, f32[2176]{0:T(1024)S(1)} %get-tuple-element.42), kind=kLoop, calls=%fused_computation.10 | loop fusion | flops 2611200 | bytes 10453504 | tf_op jit(solution)/shard_map/sub | solution.py:80
  305.0 5.5 %copy.69 = f32[2176,400]{0,1:T(8,128)} copy(f32[2176,400]{1,0:T(8,128)} %divide_subtract_fusion) | data formatting | bytes 6963200
  310.5 5.0 %copy.71 = f32[16,128,400]{2,1,0:T(8,128)} copy(f32[16,128,400]{1,2,0:T(8,128)} %all-to-all-done.2) | data formatting | bytes 6553600 | tf_op jit(solution)/shard_map/reshape | solution.py:73
  315.5 15.4 %scatter_fusion = f32[1024,400]{1,0:T(8,128)S(1)} fusion(f32[1024,400]{1,0:T(8,128)S(1)} %scatter_custom_fusion.1, s32[2048]{0:T(1024)S(1)} %bitcast.49, f32[2048,400]{1,0:T(8,128)} %bitcast.42), kind=kCustom, calls=%fused_computation.7 | custom fusion | flops 819200 | bytes 9838592 | tf_op jit(solution)/shard_map/scatter-add | solution.py:72
  334.3 2.7 copy.68
  (47 shorter events, 11.9 us)
Async XLA Ops:
  19.2 13.7 %all-to-all-start = ((s32[16,1,128]{2,1,0:T(1,128)}), s32[16,1,128]{2,1,0:T(1,128)S(1)}, u32[]{:S(2)}, u32[]{:S(2)}) async-start(s32[16,1,128]{2,1,0:T(1,128)} %bitcast.6), calls=%async_computation | async-start | bytes 16384 | tf_op jit(solution)/shard_map/all_to_all | solution.py:48
  28.5 21.6 %copy-start = (f32[1024,400]{1,0:T(8,128)}, f32[1024,400]{1,0:T(8,128)S(1)}, u32[]{:S(2)}) copy-start(f32[1024,400]{1,0:T(8,128)S(1)} %copy.64) | copy-start | bytes 4915204
  45.5 4.5 %copy-start.8 = (s32[1024]{0:T(1024)S(1)}, s32[1024]{0:T(1024)}, u32[]{:S(2)}) copy-start(s32[1024]{0:T(1024)} %param.12) | copy-start | bytes 12292
  45.5 37.6 %all-to-all-start.1 = ((bf16[16,128,400]{1,2,0:T(8,128)(2,1)}), bf16[16,128,400]{1,2,0:T(8,128)(2,1)}, u32[]{:S(2)}, u32[]{:S(2)}) async-start(bf16[16,128,400]{1,2,0:T(8,128)(2,1)} %copy.56), calls=%async_computation.1 | async-start | bytes 3276800 | tf_op jit(solution)/shard_map/all_to_all | solution.py:50
  54.9 5.3 %copy-start.9 = (s32[1024]{0:T(1024)S(1)}, s32[1024]{0:T(1024)}, u32[]{:S(2)}) copy-start(s32[1024]{0:T(1024)} %param.15) | copy-start | bytes 12292
  60.3 7.7 %copy-start.3 = (f32[1024,400]{1,0:T(8,128)S(1)}, f32[1024,400]{1,0:T(8,128)}, u32[]{:S(2)}) copy-start(f32[1024,400]{1,0:T(8,128)} %gather_fusion) | copy-start | bytes 4915204
  92.4 2.0 copy-start.2
  92.4 2.0 copy-start.6
  107.9 9.8 %copy-start.4 = (f32[1024,400]{1,0:T(8,128)S(1)}, f32[1024,400]{1,0:T(8,128)}, u32[]{:S(2)}) copy-start(f32[1024,400]{1,0:T(8,128)} %gather_fusion) | copy-start | bytes 4915204
  107.9 202.6 %all-to-all-start.2 = ((f32[16,128,400]{1,2,0:T(8,128)}), f32[16,128,400]{1,2,0:T(8,128)}, u32[]{:S(2)}, u32[]{:S(2)}) async-start(f32[16,128,400]{1,2,0:T(8,128)} %copy.61), calls=%async_computation.2 | async-start | bytes 6553600 | tf_op jit(solution)/shard_map/all_to_all | solution.py:68
  117.5 178.8 %all-reduce.2.cloned.1.call-start = ((), (), s32[]{:S(2)}) async-start(), calls=%async_computation.3 | async-start | bytes 8912896 | tf_op jit(solution)/shard_map/psum | solution.py:78
  149.5 149.6 %copy-start.7 = (f32[2176]{0:T(1024)S(1)}, f32[2176]{0:T(1024)}, u32[]{:S(2)}) copy-start(f32[2176]{0:T(1024)} %param.11) | copy-start | bytes 26116
  296.3 3.6 %copy-start.5 = (f32[2176,400]{1,0:T(8,128)S(1)}, f32[2176,400]{1,0:T(8,128)}, u32[]{:S(2)}) copy-start(f32[2176,400]{1,0:T(8,128)} %all-reduce.2.cloned.1.call-done) | copy-start | bytes 10444804
  330.9 0.7 copy-start.10
  330.9 1.6 copy-start.1
Sparse Core Ops, SparseCore 0:
  140.1 156.2 all-reduce.1
where the time goes:
time: 344 us
  waiting for transfers between devices  163 us (47%)
  local copies, waits for them, and re-layouts  80.4 us (23%)
  other arithmetic  54.8 us (16%)
  starting transfers between devices  21.7 us (6%)
  between operations  14.2 us (4%)
  matrix products  9.2 us (3%)
    psum x1, waiting for transfers between devices, on_device(): relation_grad = lax.psum(relation_terms, 'ent')  147 us
    unnamed x26, local copies, waits for them, and re-layouts  17 us
    scatter-add x1, other arithmetic, on_device(): entity_grad.at[offsets.reshape(owners * capacity)]  15.4 us
    all_to_all x1, waiting for transfers between devices, on_device(): lax.all_to_all(looked, 'ent', split_axis=0, concat_axis=0, tiled=True)  12.2 us
    gather x2, local copies, waits for them, and re-layouts, on_device(): weights = relation[rel_id]  10.4 us
    scatter-add x1, other arithmetic, on_device(): jnp.zeros(relation.shape, jnp.float32).at[rel_id].add(query_grad * sources)  9.57 us
    all_to_all x1, starting transfers between devices, on_device(): lax.all_to_all(returned, 'ent', split_axis=0, concat_axis=0, tiled=True)  9.52 us
    gather x1, local copies, waits for them, and re-layouts, on_device(): looked = entity[offsets].astype(jnp.bfloat16)  8.65 us
  transfers between devices with their start and end apart: 4, of which 3 were waited for; matrix products, arithmetic and copies ran while one was open for 20% of the time, Pallas kernels for 0%

commit v1 on v0

v1 whole, which is shorter than its diff:
```python
import functools

import jax
import jax.numpy as jnp
from jax import lax
from jax.experimental import pallas as pl
from jax.experimental.pallas import tpu as pltpu
from jax.sharding import PartitionSpec as P

BLOCK = 1024
TILE = 256
learn_rate = 0.3

f32, bf16, i32 = jnp.float32, jnp.bfloat16, jnp.int32
VM = pltpu.VMEM


def nt(a, b):
    return lax.dot_general(a, b, (((1,), (1,)), ((), ())), preferred_element_type=f32)


def tn(a, b):
    return lax.dot_general(a, b, (((0,), (0,)), ((), ())), preferred_element_type=f32)


def nn(a, b):
    return jnp.dot(a, b, preferred_element_type=f32)


def hits(first, count, row):
    return lax.broadcasted_iota(i32, (count, row.shape[1]), 0) + first == row


def ones_at(first, count, row):
    return jnp.where(hits(first, count, row), 1.0, 0.0).astype(bf16)


def tiles(total, body, size=TILE):
    whole = total // size

    def step(t, carry):
        body(pl.multiple_of(t * size, size), size)
        return carry

    lax.fori_loop(0, whole, step, 0)
    if total % size:
        body(whole * size, total % size)


def split3(x):
    high = x.astype(bf16)
    rest = x - high.astype(f32)
    mid = rest.astype(bf16)
    return high, mid, (rest - mid.astype(f32)).astype(bf16)


def rank_kernel(owners, cap, part_ref, off_ref, slot_ref, req_ref):
    part, off = part_ref[...], off_ref[...]
    edges = part.shape[1]
    mine = hits(0, owners, part)
    earlier = lax.broadcasted_iota(i32, (edges, edges), 0) < lax.broadcasted_iota(
        i32, (edges, edges), 1
    )
    before = nn(
        jnp.where(mine, 1.0, 0.0).astype(bf16), jnp.where(earlier, 1.0, 0.0).astype(bf16)
    )
    rank = jnp.sum(jnp.where(mine, before, 0.0), axis=0, keepdims=True)
    slot = part * cap + rank.astype(i32)
    slot_ref[...] = slot
    row = lax.broadcasted_iota(i32, (16, edges), 0)
    digits = jnp.where(row == 0, off >> 5, jnp.where(row == 1, off & 31, 0))
    digits = digits.astype(f32).astype(bf16)

    def body(start, width):
        found = nt(digits, ones_at(start, width, slot))
        req_ref[:, pl.ds(start, width)] = (found[0:1] * 32.0 + found[1:2]).astype(i32)

    tiles(owners * cap, body)


def lookup_kernel(cap, ent_ref, off_ref, out_ref, table):
    rows = ent_ref.shape[1]
    table[...] = ent_ref[...].astype(bf16)
    per = TILE // cap

    def step(t, carry):
        start = pl.multiple_of(t * TILE, TILE)
        off = off_ref[:, pl.ds(start, TILE)]
        got = nn(table[...], ones_at(0, rows, off)).astype(bf16)
        for j in range(per):
            out_ref[t * per + j] = got[:, j * cap : (j + 1) * cap]
        return carry

    lax.fori_loop(0, out_ref.shape[0] // per, step, 0)


def query_kernel(ent_ref, rel_ref, src_ref, rid_ref, s_ref, w_ref, q_ref, ent3, rel3):
    dim, rows = ent_ref.shape
    for into, x in ((ent3, ent_ref), (rel3, rel_ref)):
        for k, piece in enumerate(split3(x[...])):
            into[k * dim : (k + 1) * dim] = piece

    def take(table, ids):
        got = nn(table[...], ones_at(0, table.shape[1], ids))
        return got[0:dim] + got[dim : 2 * dim] + got[2 * dim :]

    def body(start, width):
        at = pl.ds(start, width)
        s = take(ent3, src_ref[:, at])
        w = take(rel3, rid_ref[:, at])
        s_ref[:, at] = s
        w_ref[:, at] = w
        q_ref[:, at] = (s * w).astype(bf16)

    tiles(src_ref.shape[1], body)


def score_kernel(cap, q_ref, t_ref, slot_ref, loss_ref, c_ref, tg_ref, tt_ref, logit, top, pos, total):
    slot = slot_ref[...]
    per = TILE // cap
    count = t_ref.shape[0] // per
    top[...] = jnp.full(top.shape, -1e30, f32)
    pos[...] = jnp.zeros(pos.shape, f32)
    total[...] = jnp.zeros(total.shape, f32)

    def first(t, carry):
        start = pl.multiple_of(t * TILE, TILE)
        block = jnp.concatenate([t_ref[t * per + j] for j in range(per)], axis=1)
        tt_ref[:, pl.ds(start, TILE)] = block
        val = tn(block, q_ref[...])
        own = hits(start, TILE, slot)
        used = jnp.max(jnp.where(own, 1.0, 0.0), axis=1, keepdims=True) > 0.5
        val = jnp.where(used, val, -1e30)
        pos[...] += jnp.sum(jnp.where(own, val, 0.0), axis=0, keepdims=True)
        top[...] = jnp.maximum(top[...], jnp.max(val, axis=0, keepdims=True))
        logit[pl.ds(start, TILE)] = val
        return carry

    lax.fori_loop(0, count, first, 0)

    def second(t, carry):
        at = pl.ds(pl.multiple_of(t * TILE, TILE), TILE)
        val = jnp.exp(logit[at] - top[...])
        total[...] += jnp.sum(val, axis=0, keepdims=True)
        logit[at] = val
        return carry

    lax.fori_loop(0, count, second, 0)
    loss_ref[...] = jnp.log(total[...]) + top[...] - pos[...]
    inverse = 1.0 / total[...]

    def third(t, carry):
        start = pl.multiple_of(t * TILE, TILE)
        at = pl.ds(start, TILE)
        prob = logit[at] * inverse
        coef = jnp.where(hits(start, TILE, slot), prob - 1.0, prob).astype(bf16)
        c_ref[at] = coef
        grad = nt(q_ref[...], coef)
        for j in range(per):
            tg_ref[t * per + j] = grad[:, j * cap : (j + 1) * cap].astype(tg_ref.dtype)
        return carry

    lax.fori_loop(0, count, third, 0)


def spread_kernel(tt_ref, c_ref, s_ref, w_ref, src_ref, rid_ref, rel_ref, ent_ref, high2, terms):
    dim = s_ref.shape[0]

    def grads(start, width):
        at = pl.ds(start, width)
        grad = nn(tt_ref[...], c_ref[:, at])
        ent = grad * w_ref[:, at]
        high = ent.astype(bf16)
        high2[0:dim, at] = high
        high2[dim : 2 * dim, at] = (ent - high.astype(f32)).astype(bf16)
        terms[:, at] = (grad * s_ref[:, at]).astype(bf16)

    tiles(s_ref.shape[1], grads)
    pad = rel_ref.shape[0] - dim

    def relation(start, width):
        at = pl.ds(start, width)
        rel_ref[0:dim, at] = nt(terms[...], ones_at(start, width, rid_ref[...])).astype(bf16)
        if pad:
            rel_ref[dim:, at] = jnp.zeros((pad, width), bf16)

    tiles(rel_ref.shape[1], relation)

    def entity(start, width):
        got = nt(high2[...], ones_at(start, width, src_ref[...]))
        ent_ref[:, pl.ds(start, width)] = got[0:dim] + got[dim:]

    tiles(ent_ref.shape[1], entity)


def sum_kernel(owners, chunk, x_ref, out_ref, acc, *rest):
    steps = owners.bit_length() - 1
    boxes = rest[:steps]
    send1, recv1, send2, recv2 = rest[steps:]
    me = lax.axis_index("ent")
    bit = [(me // 2**k) % 2 for k in range(steps)]
    mate = [me + (1 - 2 * bit[k]) * 2**k for k in range(steps)]
    barrier = pltpu.get_barrier_semaphore()
    for k in range(steps):
        pl.semaphore_signal(
            barrier, inc=1, device_id={"ent": mate[k]}, device_id_type=pl.DeviceIdType.MESH
        )
    pl.semaphore_wait(barrier, steps)
    low = 0
    size = owners * chunk
    lows = []
    for k in range(steps):
        lows.append((low, size))
        half = size // 2
        keep = pl.multiple_of(low + bit[k] * half, chunk)
        give = pl.multiple_of(low + (1 - bit[k]) * half, chunk)
        source = x_ref if k == 0 else acc
        copy = pltpu.make_async_remote_copy(
            src_ref=source.at[pl.ds(give, half)],
            dst_ref=boxes[k],
            send_sem=send1.at[k],
            recv_sem=recv1.at[k],
            device_id={"ent": mate[k]},
            device_id_type=pl.DeviceIdType.MESH,
        )
        copy.start()
        copy.wait()
        into = out_ref if k == steps - 1 else acc
        into[pl.ds(keep, half)] = (
            source[pl.ds(keep, half)].astype(f32) + boxes[k][...].astype(f32)
        ).astype(bf16)
        low, size = keep, half
    for k in reversed(range(steps)):
        whole = lows[k][1]
        half = whole // 2
        at = pl.multiple_of(lows[k][0] + bit[k] * half, chunk)
        copy = pltpu.make_async_remote_copy(
            src_ref=out_ref.at[pl.ds(at, half)],
            dst_ref=out_ref.at[pl.ds(at, half)],
            send_sem=send2.at[k],
            recv_sem=recv2.at[k],
            device_id={"ent": mate[k]},
            device_id_type=pl.DeviceIdType.MESH,
        )
        copy.start()
        copy.wait()


def step_rows(value, state, grad):
    after = state + jnp.sum(grad * grad, axis=0, keepdims=True) * (1.0 / grad.shape[0])
    return value - grad * (learn_rate / jnp.sqrt(after)), after


def entity_kernel(cap, arr_ref, off_ref, part_ref, ent_ref, state_ref, new_ref, after_ref, both):
    dim = ent_ref.shape[0]
    per = TILE // cap

    def load(t, carry):
        at = pl.ds(pl.multiple_of(t * TILE, TILE), TILE)
        got = jnp.concatenate([arr_ref[t * per + j] for j in range(per)], axis=1)
        high = got.astype(bf16)
        both[0:dim, at] = high
        both[dim:, at] = (got - high.astype(f32)).astype(bf16)
        return carry

    lax.fori_loop(0, arr_ref.shape[0] // per, load, 0)

    def body(start, width):
        at = pl.ds(start, width)
        got = nt(both[...], ones_at(start, width, off_ref[...]))
        grad = got[0:dim] + got[dim:] + part_ref[:, at]
        new_ref[:, at], after_ref[:, at] = step_rows(ent_ref[:, at], state_ref[:, at], grad)

    tiles(ent_ref.shape[1], body)


def relation_kernel(grad_ref, rel_ref, state_ref, new_ref, after_ref):
    dim = rel_ref.shape[0]

    def body(start, width):
        at = pl.ds(start, width)
        grad = grad_ref[0:dim, at].astype(f32)
        new_ref[:, at], after_ref[:, at] = step_rows(rel_ref[:, at], state_ref[:, at], grad)

    tiles(rel_ref.shape[1], body)


def call(kernel, outs, scratch=(), flops=0, moved=0, **extra):
    shapes = [jax.ShapeDtypeStruct(shape, kind) for shape, kind in outs]
    return pl.pallas_call(
        kernel,
        out_shape=shapes,
        scratch_shapes=list(scratch),
        cost_estimate=pl.CostEstimate(flops=flops, bytes_accessed=moved, transcendentals=0),
        compiler_params=pltpu.CompilerParams(vmem_limit_bytes=48 * 2**20, **extra),
    )


def on_device(
    entity, entity_state, relation, relation_state, src_offset, dst_part, dst_offset, rel_id
):
    rows, dim = entity.shape
    nrel = relation.shape[0]
    edges = src_offset.shape[0]
    assert edges == BLOCK
    owners = lax.axis_size("ent")
    cap = max(2, 2 * edges // owners)
    slots = owners * cap
    chunk = -(-dim // (owners * 16)) * 16
    ent_t, rel_t = entity.T, relation.T
    as_row = lambda x: x.reshape(1, -1)
    src, rid = as_row(src_offset), as_row(rel_id)
    mac = lambda a, b, c: 2 * a * b * c

    slot, requests = call(
        functools.partial(rank_kernel, owners, cap),
        [((1, edges), i32), ((1, slots), i32)],
        flops=mac(16, slots, edges),
        moved=slots * 8,
    )(as_row(dst_part), as_row(dst_offset))
    offsets = lax.all_to_all(
        requests.reshape(owners, cap), "ent", split_axis=0, concat_axis=0, tiled=True
    )
    offsets = as_row(offsets)
    (looked,) = call(
        functools.partial(lookup_kernel, cap),
        [((owners, dim, cap), bf16)],
        [VM((dim, rows), bf16)],
        flops=mac(dim, rows, slots),
        moved=dim * rows * 4,
    )(ent_t, offsets)
    replies = lax.all_to_all(looked, "ent", split_axis=0, concat_axis=0, tiled=True)
    sources, weights, queries = call(
        query_kernel,
        [((dim, edges), f32), ((dim, edges), f32), ((dim, edges), bf16)],
        [VM((3 * dim, rows), bf16), VM((3 * dim, nrel), bf16)],
        flops=mac(3 * dim, rows + nrel, edges),
        moved=dim * nrel * 4,
    )(ent_t, rel_t, src, rid)
    edge_loss, coef, target_grad, targets = call(
        functools.partial(score_kernel, cap),
        [((1, edges), f32), ((slots, edges), bf16), ((owners, dim, cap), f32), ((dim, slots), bf16)],
        [VM((slots, edges), f32)] + [VM((1, edges), f32)] * 3,
        flops=mac(2 * dim, slots, edges),
        moved=slots * edges * 2,
    )(queries, replies, slot)
    arrived = lax.all_to_all(target_grad, "ent", split_axis=0, concat_axis=0, tiled=True)
    relation_terms, entity_part = call(
        spread_kernel,
        [((owners * chunk, nrel), bf16), ((dim, rows), f32)],
        [VM((2 * dim, edges), bf16), VM((dim, edges), bf16)],
        flops=mac(dim, edges, slots + nrel + 2 * rows),
        moved=dim * nrel * 2,
    )(targets, coef, sources, weights, src, rid)
    steps = owners.bit_length() - 1
    (relation_grad,) = call(
        functools.partial(sum_kernel, owners, chunk),
        [((owners * chunk, nrel), bf16)],
        [VM((owners * chunk, nrel), bf16)]
        + [VM(((owners * chunk) >> (k + 1), nrel), bf16) for k in range(steps)]
        + [pltpu.SemaphoreType.DMA((steps,))] * 4,
        moved=dim * nrel * 8,
        collective_id=0,
        has_side_effects=True,
    )(relation_terms)
    new_rel, rel_after = call(
        relation_kernel, [((dim, nrel), f32), ((1, nrel), f32)], moved=dim * nrel * 10
    )(relation_grad, rel_t, as_row(relation_state))
    new_ent, ent_after = call(
        functools.partial(entity_kernel, cap),
        [((dim, rows), f32), ((1, rows), f32)],
        [VM((2 * dim, slots), bf16)],
        flops=mac(2 * dim, slots, rows),
        moved=dim * rows * 8,
    )(arrived, offsets, entity_part, ent_t, as_row(entity_state))
    return (
        new_ent.T,
        ent_after.reshape(rows),
        new_rel.T,
        rel_after.reshape(nrel),
        edge_loss.reshape(edges),
    )


def solution(mesh):
    placed = (
        P(("groups", "ent"), None),
        P(("groups", "ent")),
        P("groups", None),
        P("groups"),
        P(("groups", "ent")),
        P(("groups", "ent"), None),
        P(("groups", "ent")),
        P(("groups", "ent")),
    )
    return jax.shard_map(
        on_device,
        mesh=mesh,
        in_specs=placed,
        out_specs=(
            P(("groups", "ent"), None),
            P(("groups", "ent")),
            P("groups", None),
            P("groups"),
            P(("groups", "ent")),
        ),
        check_vma=False,
    )
```

time: 344 us -> 207 us (0.60)
  Pallas kernels: 0 us -> 146 us
  waiting for transfers between devices: 163 us -> 17.4 us
  local copies, waits for them, and re-layouts: 80.4 us -> 14 us
  other arithmetic: 54.8 us -> 0.63 us
  blocking collectives: 0 us -> 13.6 us
  between operations: 14.2 us -> 0.77 us
  matrix products: 9.2 us -> 0 us
  starting transfers between devices: 21.7 us -> 13.4 us
    psum x1 -> x0, waiting for transfers between devices: 147 us -> none  [on_device(): relation_grad = lax.psum(relation_terms, 'ent')]
    pallas_call x0 -> x8, Pallas kernels: none -> 146 us  [the longest x1 91.6 us: on_device(): call(functools.partial(sum_kernel, owners, chunk), [((owners * chunk, nre...]
    scatter-add x3 -> x0, other arithmetic: 32.7 us -> none  [the longest x1 15.4 us: on_device(): entity_grad.at[offsets.reshape(owners * capacity)]]
    gather x6 -> x0, local copies, waits for them, and re-layouts: 29.6 us -> none  [the longest x2 10.4 us: on_device(): weights = relation[rel_id]]
    all_to_all x0 -> x1, blocking collectives: none -> 13.6 us  [on_device(): lax.all_to_all(requests.reshape(owners, cap), 'ent', split_axis=0, concat...]
    scatter x2 -> x0, local copies, waits for them, and re-layouts: 12.1 us -> none  [the longest x1 7.01 us: on_device(): jnp.zeros((owners * capacity, feat_dim), jnp.float32).at[slot_index]]
    reshape x2 -> x1, local copies, waits for them, and re-layouts: 10.3 us -> 0.01 us  [on_device(): as_row = lambda x: x.reshape(1, -1)]
    dot_general x3 -> x0, matrix products: 9.2 us -> none  [the longest x1 5.42 us: score_one(): jnp.dot(coefficient, target_block, preferred_element_type=jnp.float32)]
  transfers between devices with their start and end apart: 4 -> 2, of which waited for: 3 -> 1; matrix products, arithmetic and copies ran while one was open for 20% -> 0% of each run, Pallas kernels for 0% -> 58%
where the time goes in v1:
time: 207 us; the launch traced here: 206 us
  Pallas kernels  146 us (71%)
  waiting for transfers between devices  17.4 us (8%)
  local copies, waits for them, and re-layouts  14 us (7%)
  blocking collectives  13.6 us (7%)
  starting transfers between devices  13.4 us (6%)
    pallas_call x1, Pallas kernels, on_device(): call(functools.partial(sum_kernel, owners, chunk), [((owners * chunk, nre...  91.6 us
    all_to_all x1, waiting for transfers between devices, on_device(): lax.all_to_all(looked, 'ent', split_axis=0, concat_axis=0, tiled=True)  17.4 us
    unnamed x38, local copies, waits for them, and re-layouts  14 us
    all_to_all x1, blocking collectives, on_device(): lax.all_to_all(requests.reshape(owners, cap), 'ent', split_axis=0, concat...  13.6 us
    pallas_call x1, Pallas kernels, on_device(): call(functools.partial(score_kernel, cap), [((1, edges), f32), ((slots, e...  12.4 us
    pallas_call x1, Pallas kernels, on_device(): call(query_kernel, [((dim, edges), f32), ((dim, edges), f32), ((dim, edge...  12.3 us
    pallas_call x1, Pallas kernels, on_device(): call(spread_kernel, [((owners * chunk, nrel), bf16), ((dim, rows), f32)],...  12.2 us
    all_to_all x1, starting transfers between devices, on_device(): lax.all_to_all(target_grad, 'ent', split_axis=0, concat_axis=0, tiled=True)  9.52 us
  transfers between devices with their start and end apart: 2, of which 1 were waited for; matrix products, arithmetic and copies ran while one was open for 0% of the time, Pallas kernels for 58%

profile of v1, /device:TPU:0, one launch (start us, length us, event | category | flops | bytes accessed | tf_op | source)
XLA Modules:
  0.0 206.3 jit_solution(4450145102271756605)
XLA Ops:
  0.6 0.0 copy-start.4
  0.6 0.7 copy-done.4
  1.3 0.7 copy-done.5
  2.0 2.5 %shard_map.120 = (s32[1,1024]{1,0:T(1,128)S(1)}, s32[1,2048]{1,0:T(1,128)S(1)}) custom-call(s32[1,1024]{1,0:T(1,128)S(1)} %bitcast.23, s32[1,1024]{1,0:T(1,128)S(1)} %bitcast.24), custom_call_target="tpu_custom_call" | custom-call | flops 67108864 | bytes 16384 | tf_op jit(solution)/shard_map/pallas_call | solution.py:315
  4.5 13.6 %all_to_all.19 = s32[16,1,128]{2,1,0:T(1,128)S(1)} all-to-all(s32[16,1,128]{2,1,0:T(1,128)S(1)} %bitcast.19), channel_id=1, replica_groups=mesh['groups'=2,'ent'=16] {'ent'}, dimensions={0} | all-to-all | bytes 16384 | tf_op jit(solution)/shard_map/all_to_all | solution.py:321
  18.1 1.4 copy-done.2
  19.5 4.3 %shard_map.121 = bf16[16,400,128]{2,1,0:T(8,128)(2,1)} custom-call(f32[400,1024]{1,0:T(8,128)S(1)} %bitcast.20, s32[1,2048]{1,0:T(1,128)S(1)} %bitcast.17), custom_call_target="tpu_custom_call" | custom-call | flops 1677721600 | bytes 1638400 | tf_op jit(solution)/shard_map/pallas_call | solution.py:325
  23.8 3.8 %all-to-all-start.1 = ((bf16[16,400,128]{2,1,0:T(8,128)(2,1)}), bf16[16,400,128]{2,1,0:T(8,128)(2,1)S(1)}, u32[]{:S(2)}, u32[]{:S(2)}) async-start(bf16[16,400,128]{2,1,0:T(8,128)(2,1)} %shard_map.121), calls=%async_computation.1 | async-start | bytes 3276800 | tf_op jit(solution)/shard_map/all_to_all | solution.py:332
  27.7 12.3 %shard_map.119 = (f32[400,1024]{1,0:T(8,128)S(1)}, f32[400,1024]{1,0:T(8,128)S(1)}, bf16[400,1024]{1,0:T(8,128)(2,1)S(1)}) custom-call(f32[400,1024]{1,0:T(8,128)S(1)} %bitcast.21, f32[400,2176]{1,0:T(8,128)} %bitcast.15, s32[1,1024]{1,0:T(1,128)S(1)} %bitcast.25, s32[1,1024]{1,0:T(1,128)S(1)} %bitcast.27), custom_call_target="tpu_custom_call" | custom-call | flops 7864320000 | bytes 3481600 | tf_op jit(solution)/shard_map/pallas_call | solution.py:333
  40.1 0.0 copy-start.11
  40.1 1.2 copy-done.11
  41.2 1.2 copy-done.13
  42.4 0.9 copy-done.16
  43.3 17.4 %all-to-all-done.1.t_ref = bf16[16,400,128]{2,1,0:T(8,128)(2,1)S(1)} async-done(((bf16[16,400,128]{2,1,0:T(8,128)(2,1)}), bf16[16,400,128]{2,1,0:T(8,128)(2,1)S(1)}, u32[]{:S(2)}, u32[]{:S(2)}) %all-to-all-start.1) | async-done | bytes 1638432 | tf_op jit(solution)/shard_map/all_to_all | solution.py:332
  60.7 1.1 copy-done.17
  61.9 12.4 %shard_map.122 = (f32[1,1024]{1,0:T(1,128)}, bf16[2048,1024]{1,0:T(8,128)(2,1)}, f32[16,400,128]{2,1,0:T(8,128)}, bf16[400,2048]{1,0:T(8,128)(2,1)S(1)}) custom-call(bf16[400,1024]{1,0:T(8,128)(2,1)S(1)} %copy-done.17, bf16[16,400,128]{2,1,0:T(8,128)(2,1)S(1)} %all-to-all-done.1.t_ref, s32[1,1024]{1,0:T(1,128)S(1)} %get-tuple-element.22.slot_ref), custom_call_target="tpu_custom_call" | custom-call | flops 3355443200 | bytes 4194304 | tf_op jit(solution)/shard_map/pallas_call | solution.py:340
  74.3 1.2 copy-done.14
  75.4 9.5 %all-to-all-start.2 = ((f32[16,400,128]{2,1,0:T(8,128)}), f32[16,400,128]{2,1,0:T(8,128)}, u32[]{:S(2)}, u32[]{:S(2)}) async-start(f32[16,400,128]{2,1,0:T(8,128)} %get-tuple-element.23), calls=%async_computation.2 | async-start | bytes 6553600 | tf_op jit(solution)/shard_map/all_to_all | solution.py:347
  85.0 0.0 copy-done.18
  85.0 0.0 copy-start.15
  85.0 1.4 copy-done.15
  86.4 12.2 %shard_map.123 = (bf16[512,2176]{1,0:T(8,128)(2,1)}, f32[400,1024]{1,0:T(8,128)S(1)}) custom-call(bf16[400,2048]{1,0:T(8,128)(2,1)S(1)} %copy-done.15, bf16[2048,1024]{1,0:T(8,128)(2,1)} %get-tuple-element.25.c_ref, f32[400,1024]{1,0:T(8,128)S(1)} %copy-done.12, f32[400,1024]{1,0:T(8,128)} %copy-done.13, s32[1,1024]{1,0:T(1,128)S(1)} %bitcast.26, ...), custom_call_target="tpu_custom_call" | custom-call | flops 5138022400 | bytes 1740800 | tf_op jit(solution)/shard_map/pallas_call | solution.py:348
  98.6 1.2 copy-done.9
  99.8 1.6 copy-done.1
  101.4 91.6 %shard_map.125.grad_ref = bf16[512,2176]{1,0:T(8,128)(2,1)S(1)} custom-call(bf16[512,2176]{1,0:T(8,128)(2,1)S(1)} %copy-done.1), custom_call_target="tpu_custom_call" | custom-call | bytes 6963200 | tf_op jit(solution)/shard_map/pallas_call | solution.py:356
  193.0 0.0 copy-done
  193.0 0.0 copy-start.8
  193.0 2.9 %shard_map.126 = (f32[400,2176]{1,0:T(8,128)}, f32[1,2176]{1,0:T(1,128)S(1)}) custom-call(bf16[512,2176]{1,0:T(8,128)(2,1)S(1)} %shard_map.125.grad_ref, f32[400,2176]{1,0:T(8,128)S(1)} %bitcast.16, f32[1,2176]{1,0:T(1,128)S(1)} %reshape.52.state_ref), custom_call_target="tpu_custom_call" | custom-call | bytes 8704000 | tf_op jit(solution)/shard_map/pallas_call | solution.py:366
  195.9 0.6 reduce
  196.6 0.0 all-to-all-done.2.arr_ref
  196.6 1.4 copy-done.10
  198.0 8.3 %shard_map.124 = (f32[400,1024]{1,0:T(8,128)}, f32[1,1024]{1,0:T(1,128)}) custom-call(f32[16,400,128]{2,1,0:T(8,128)} %all-to-all-done.2.arr_ref, s32[1,2048]{1,0:T(1,128)S(1)} %bitcast.18, f32[400,1024]{1,0:T(8,128)S(1)} %copy-done.10, f32[400,1024]{1,0:T(8,128)S(1)} %bitcast.22, f32[1,1024]{1,0:T(1,128)S(1)} %bitcast.29), custom_call_target="tpu_custom_call" | custom-call | flops 3355443200 | bytes 3276800 | tf_op jit(solution)/shard_map/pallas_call | solution.py:369
  (21 shorter events, 0.0 us)
Async XLA Ops:
  0.6 0.7 copy-start.4
  1.3 0.7 copy-start.5
  18.1 1.4 copy-start.2
  23.8 3.9 %copy-start.3 = (f32[1024,400]{0,1:T(8,128)S(1)}, f32[1024,400]{0,1:T(8,128)}, u32[]{:S(2)}) copy-start(f32[1024,400]{0,1:T(8,128)} %param.8) | copy-start | bytes 4915204
  23.8 3.9 %copy-start.6 = (s32[1024]{0:T(1024)S(1)}, s32[1024]{0:T(1024)}, u32[]{:S(2)}) copy-start(s32[1024]{0:T(1024)} %param.12) | copy-start | bytes 12292
  23.8 3.9 %copy-start.7 = (s32[1024]{0:T(1024)S(1)}, s32[1024]{0:T(1024)}, u32[]{:S(2)}) copy-start(s32[1024]{0:T(1024)} %param.15) | copy-start | bytes 12292
  23.8 36.9 %all-to-all-start.1 = ((bf16[16,400,128]{2,1,0:T(8,128)(2,1)}), bf16[16,400,128]{2,1,0:T(8,128)(2,1)S(1)}, u32[]{:S(2)}, u32[]{:S(2)}) async-start(bf16[16,400,128]{2,1,0:T(8,128)(2,1)} %shard_map.121), calls=%async_computation.1 | async-start | bytes 3276800 | tf_op jit(solution)/shard_map/all_to_all | solution.py:332
  40.1 1.2 copy-start.11
  41.2 1.2 copy-start.13
  42.4 0.9 copy-start.16
  60.7 1.1 copy-start.17
  74.3 1.2 copy-start.14
  75.4 9.5 %copy-start.18 = (f32[2176]{0:T(1024)S(1)}, f32[2176]{0:T(1024)}, u32[]{:S(2)}) copy-start(f32[2176]{0:T(1024)} %param.11) | copy-start | bytes 26116
  75.4 9.6 %copy-start.12 = (f32[400,1024]{1,0:T(8,128)S(1)}, f32[400,1024]{1,0:T(8,128)}, u32[]{:S(2)}) copy-start(f32[400,1024]{1,0:T(8,128)} %copy-done.11) | copy-start | bytes 4915204
  75.4 121.1 %all-to-all-start.2 = ((f32[16,400,128]{2,1,0:T(8,128)}), f32[16,400,128]{2,1,0:T(8,128)}, u32[]{:S(2)}, u32[]{:S(2)}) async-start(f32[16,400,128]{2,1,0:T(8,128)} %get-tuple-element.23), calls=%async_computation.2 | async-start | bytes 6553600 | tf_op jit(solution)/shard_map/all_to_all | solution.py:347
  85.0 1.4 copy-start.15
  98.6 1.2 copy-start.9
  99.8 1.6 copy-start.1
  101.4 91.6 %copy-start = (f32[2176,400]{0,1:T(8,128)S(1)}, f32[2176,400]{0,1:T(8,128)}, u32[]{:S(2)}) copy-start(f32[2176,400]{0,1:T(8,128)} %param.10) | copy-start | bytes 10444804
  193.0 3.6 %copy-start.8 = (f32[1024]{0:T(1024)S(1)}, f32[1024]{0:T(1024)}, u32[]{:S(2)}) copy-start(f32[1024]{0:T(1024)} %param.9) | copy-start | bytes 12292
  196.6 1.4 copy-start.10

commit v2 on v1

v2 whole, which is shorter than its diff:
```python
import functools

import jax
import jax.numpy as jnp
from jax import lax
from jax.experimental import pallas as pl
from jax.experimental.pallas import tpu as pltpu
from jax.sharding import PartitionSpec as P

BLOCK = 1024
TILE = 256
learn_rate = 0.3

f32, bf16, i32 = jnp.float32, jnp.bfloat16, jnp.int32
VM = pltpu.VMEM


def nt(a, b):
    return lax.dot_general(a, b, (((1,), (1,)), ((), ())), preferred_element_type=f32)


def tn(a, b):
    return lax.dot_general(a, b, (((0,), (0,)), ((), ())), preferred_element_type=f32)


def nn(a, b):
    return jnp.dot(a, b, preferred_element_type=f32)


def hits(first, count, row):
    return lax.broadcasted_iota(i32, (count, row.shape[1]), 0) + first == row


def ones_at(first, count, row):
    return jnp.where(hits(first, count, row), 1.0, 0.0).astype(bf16)


def tiles(total, body, size=TILE):
    whole = total // size

    def step(t, carry):
        body(pl.multiple_of(t * size, size), size)
        return carry

    lax.fori_loop(0, whole, step, 0)
    if total % size:
        body(whole * size, total % size)


def split3(x):
    high = x.astype(bf16)
    rest = x - high.astype(f32)
    mid = rest.astype(bf16)
    return high, mid, (rest - mid.astype(f32)).astype(bf16)


MESH = pl.DeviceIdType.MESH


def greet(owners, me):
    barrier = pltpu.get_barrier_semaphore()

    def step(d, carry):
        pl.semaphore_signal(
            barrier, inc=1, device_id={"ent": (me + d) % owners}, device_id_type=MESH
        )
        return carry

    lax.fori_loop(1, owners, step, 0)
    return barrier


def swap(owners, me, source, target, send, recv):
    def copy(d):
        other = (me + d) % owners
        return pltpu.make_async_remote_copy(
            src_ref=source.at[other],
            dst_ref=target.at[me],
            send_sem=send.at[d],
            recv_sem=recv.at[d],
            device_id={"ent": other},
            device_id_type=MESH,
        )

    return copy


def each_peer(owners, body):
    def step(t, carry):
        body(1 + (owners // 2 - 1 + t) % (owners - 1))
        return carry

    lax.fori_loop(0, owners - 1, step, 0)


def fetch_kernel(
    owners, cap, part_ref, off_ref, ent_ref, rel_ref, src_ref, rid_ref,
    slot_ref, asked_ref, t_ref, s_ref, w_ref, q_ref,
    request, found, ent3, rel3, send1, recv1, send2, recv2,
):
    me = lax.axis_index("ent")
    barrier = greet(owners, me)
    dim, rows = ent_ref.shape
    part, off = part_ref[...], off_ref[...]
    edges = part.shape[1]
    mine = hits(0, owners, part)
    earlier = lax.broadcasted_iota(i32, (edges, edges), 0) < lax.broadcasted_iota(
        i32, (edges, edges), 1
    )
    before = nn(
        jnp.where(mine, 1.0, 0.0).astype(bf16), jnp.where(earlier, 1.0, 0.0).astype(bf16)
    )
    rank = jnp.sum(jnp.where(mine, before, 0.0), axis=0, keepdims=True)
    slot = part * cap + rank.astype(i32)
    slot_ref[...] = slot
    row = lax.broadcasted_iota(i32, (16, edges), 0)
    digits = jnp.where(row == 0, off >> 5, jnp.where(row == 1, off & 31, 0))
    digits = digits.astype(f32).astype(bf16)
    per = TILE // cap

    def ask(t, carry):
        got = nt(digits, ones_at(t * TILE, TILE, slot))
        got = (got[0:1] * 32.0 + got[1:2]).astype(i32)
        for j in range(per):
            request[t * per + j] = jnp.broadcast_to(got[:, j * cap : (j + 1) * cap], (8, cap))
        return carry

    lax.fori_loop(0, owners // per, ask, 0)
    pl.semaphore_wait(barrier, owners - 1)
    ids = swap(owners, me, request, asked_ref, send1, recv1)
    each_peer(owners, lambda d: ids(d).start())
    asked_ref[me] = request[me]
    for k, piece in enumerate(split3(ent_ref[...])):
        ent3[k * dim : (k + 1) * dim] = piece

    def look(owner):
        found[owner] = nn(ent3[0:dim], ones_at(0, rows, asked_ref[owner][0:1])).astype(bf16)

    each_peer(owners, lambda d: ids(d).wait())
    rows_out = swap(owners, me, found, t_ref, send2, recv2)

    def reply(d):
        look((me + d) % owners)
        rows_out(d).start()

    each_peer(owners, reply)
    look(me)
    t_ref[me] = found[me]

    for k, piece in enumerate(split3(rel_ref[...])):
        rel3[k * dim : (k + 1) * dim] = piece

    def take(table, ids_row):
        got = nn(table[...], ones_at(0, table.shape[1], ids_row))
        return got[0:dim] + got[dim : 2 * dim] + got[2 * dim :]

    def body(start, width):
        at = pl.ds(start, width)
        s = take(ent3, src_ref[:, at])
        w = take(rel3, rid_ref[:, at])
        s_ref[:, at] = s
        w_ref[:, at] = w
        q_ref[:, at] = (s * w).astype(bf16)

    tiles(edges, body)
    each_peer(owners, lambda d: rows_out(d).wait())


def quantum(power):
    return jnp.exp2(power) * (1.0 / 32000.0)


def encode(x):
    power = jnp.ceil(jnp.log2(jnp.maximum(jnp.max(jnp.abs(x), axis=0, keepdims=True), 1e-30)))
    return jnp.floor(x * (1.0 / quantum(power)) + 0.5), power


def short(x):
    return x.astype(i32).astype(jnp.int16)


def wide(x):
    return x.astype(i32).astype(f32)


def score_kernel(cap, q_ref, t_ref, slot_ref, loss_ref, c_ref, tg_ref, tt_ref, logit, top, pos, total):
    slot = slot_ref[...]
    per = TILE // cap
    count = t_ref.shape[0] // per
    top[...] = jnp.full(top.shape, -1e30, f32)
    pos[...] = jnp.zeros(pos.shape, f32)
    total[...] = jnp.zeros(total.shape, f32)

    def first(t, carry):
        start = pl.multiple_of(t * TILE, TILE)
        block = jnp.concatenate([t_ref[t * per + j] for j in range(per)], axis=1)
        tt_ref[:, pl.ds(start, TILE)] = block
        val = tn(block, q_ref[...])
        own = hits(start, TILE, slot)
        used = jnp.max(jnp.where(own, 1.0, 0.0), axis=1, keepdims=True) > 0.5
        val = jnp.where(used, val, -1e30)
        pos[...] += jnp.sum(jnp.where(own, val, 0.0), axis=0, keepdims=True)
        top[...] = jnp.maximum(top[...], jnp.max(val, axis=0, keepdims=True))
        logit[pl.ds(start, TILE)] = val
        return carry

    lax.fori_loop(0, count, first, 0)

    def second(t, carry):
        at = pl.ds(pl.multiple_of(t * TILE, TILE), TILE)
        val = jnp.exp(logit[at] - top[...])
        total[...] += jnp.sum(val, axis=0, keepdims=True)
        logit[at] = val
        return carry

    lax.fori_loop(0, count, second, 0)
    loss_ref[...] = jnp.log(total[...]) + top[...] - pos[...]
    inverse = 1.0 / total[...]

    def third(t, carry):
        start = pl.multiple_of(t * TILE, TILE)
        at = pl.ds(start, TILE)
        prob = logit[at] * inverse
        coef = jnp.where(hits(start, TILE, slot), prob - 1.0, prob).astype(bf16)
        c_ref[at] = coef
        grad, power = encode(nt(q_ref[...], coef))
        code = short(jnp.concatenate([grad, jnp.broadcast_to(power, (16, TILE))], axis=0))
        for j in range(per):
            tg_ref[t * per + j] = code[:, j * cap : (j + 1) * cap]
        return carry

    lax.fori_loop(0, count, third, 0)


def return_kernel(
    owners, cap, share, tg_ref, tt_ref, c_ref, s_ref, w_ref, src_ref, rid_ref, asked_ref,
    ent_ref, state_ref, new_ref, after_ref, out_ref,
    arrived, high2, terms2, acc, part, both, *rest,
):
    steps = owners.bit_length() - 1
    boxes, bags = rest[:steps], rest[steps : 2 * steps]
    send0, recv0, send1, recv1, send2, recv2 = rest[2 * steps :]
    me = lax.axis_index("ent")
    barrier = greet(owners, me)
    pl.semaphore_wait(barrier, owners - 1)
    grads_out = swap(owners, me, tg_ref, arrived, send0, recv0)
    each_peer(owners, lambda d: grads_out(d).start())
    arrived[me] = tg_ref[me]

    dim, edges = s_ref.shape
    chunk = acc.shape[1]

    def halves(into, at, x):
        high = x.astype(bf16)
        into[0:dim, at] = high
        into[dim : 2 * dim, at] = (x - high.astype(f32)).astype(bf16)

    def grads(start, width):
        at = pl.ds(start, width)
        grad = nn(tt_ref[...], c_ref[:, at])
        halves(high2, at, grad * w_ref[:, at])
        halves(terms2, at, grad * s_ref[:, at])

    tiles(edges, grads)

    def relation(start, width):
        at = pl.ds(start, width)
        got = nt(terms2[...], ones_at(start, width, rid_ref[...]))
        got = got[0:dim] + got[dim:]
        for c in range(owners):
            low, high = min(c * share, dim), min((c + 1) * share, dim)
            gap = jnp.zeros((chunk - (high - low), width), f32)
            acc[c, :, at] = jnp.concatenate([got[low:high], gap], axis=0) if high > low else gap

    tiles(acc.shape[2], relation)

    def pack(c):
        code, power = encode(acc[c])
        last = lax.broadcasted_iota(i32, code.shape, 0) == chunk - 1
        return short(jnp.where(last, power, code))

    def entity_part(start, width):
        got = nt(high2[...], ones_at(start, width, src_ref[...]))
        part[:, pl.ds(start, width)] = got[0:dim] + got[dim:]

    def entity_all():
        each_peer(owners, lambda d: grads_out(d).wait())
        per = TILE // cap

        def load(t, carry):
            got = jnp.concatenate([arrived[t * per + j] for j in range(per)], axis=1)
            got = wide(got)
            got = got[0:dim] * quantum(got[dim : dim + 1])
            halves(both, pl.ds(pl.multiple_of(t * TILE, TILE), TILE), got)
            return carry

        lax.fori_loop(0, owners // per, load, 0)
        asked = jnp.concatenate([asked_ref[p][0:1] for p in range(owners)], axis=1)

        def body(start, width):
            at = pl.ds(start, width)
            got = nt(both[...], ones_at(start, width, asked))
            grad = got[0:dim] + got[dim:] + part[:, at]
            new_ref[:, at], after_ref[:, at] = step_rows(ent_ref[:, at], state_ref[:, at], grad)

        tiles(ent_ref.shape[1], body)

    def remote(source, target, mate, send, recv):
        return pltpu.make_async_remote_copy(
            src_ref=source, dst_ref=target, send_sem=send, recv_sem=recv,
            device_id={"ent": mate}, device_id_type=MESH,
        )

    bit = [(me // 2**k) % 2 for k in range(steps)]
    mate = [me + (1 - 2 * bit[k]) * 2**k for k in range(steps)]
    low, size, lows = 0, owners, []
    for k in range(steps):
        lows.append((low, size))
        half = size // 2
        keep, give = low + bit[k] * half, low + (1 - bit[k]) * half

        def fill(c, carry):
            bags[k][c] = pack(give + c)
            return carry

        lax.fori_loop(0, half, fill, 0)
        copy = remote(bags[k], boxes[k], mate[k], send1.at[k], recv1.at[k])
        copy.start()
        if k == 0:
            tiles(ent_ref.shape[1], entity_part)
        copy.wait()

        def add(c, carry):
            got = wide(boxes[k][c])
            body = got * quantum(got[chunk - 1 :])
            last = lax.broadcasted_iota(i32, got.shape, 0) == chunk - 1
            acc[keep + c] = acc[keep + c] + jnp.where(last, 0.0, body)
            return carry

        lax.fori_loop(0, half, add, 0)
        low, size = keep, half
    out_ref[low] = pack(low)
    for k in reversed(range(steps)):
        half = lows[k][1] // 2
        place = out_ref.at[pl.ds(lows[k][0] + bit[k] * half, half)]
        copy = remote(place, place, mate[k], send2.at[k], recv2.at[k])
        copy.start()
        if k == min(1, steps - 1):
            entity_all()
        copy.wait()


def step_rows(value, state, grad):
    after = state + jnp.sum(grad * grad, axis=0, keepdims=True) * (1.0 / grad.shape[0])
    return value - grad * (learn_rate / jnp.sqrt(after)), after


def relation_kernel(share, code_ref, rel_ref, state_ref, new_ref, after_ref):
    dim = rel_ref.shape[0]

    def body(start, width):
        at = pl.ds(start, width)
        pieces = []
        for c in range(-(-dim // share)):
            got = wide(code_ref[c, :, at])
            used = min(share, dim - c * share)
            pieces.append(got[0:used] * quantum(got[code_ref.shape[1] - 1 :]))
        grad = jnp.concatenate(pieces, axis=0)
        new_ref[:, at], after_ref[:, at] = step_rows(rel_ref[:, at], state_ref[:, at], grad)

    tiles(rel_ref.shape[1], body)


def call(kernel, outs, scratch=(), flops=0, moved=0, **extra):
    shapes = [jax.ShapeDtypeStruct(shape, kind) for shape, kind in outs]
    return pl.pallas_call(
        kernel,
        out_shape=shapes,
        scratch_shapes=list(scratch),
        cost_estimate=pl.CostEstimate(flops=flops, bytes_accessed=moved, transcendentals=0),
        compiler_params=pltpu.CompilerParams(vmem_limit_bytes=56 * 2**20, **extra),
    )


def on_device(
    entity, entity_state, relation, relation_state, src_offset, dst_part, dst_offset, rel_id
):
    rows, dim = entity.shape
    nrel = relation.shape[0]
    edges = src_offset.shape[0]
    assert edges == BLOCK
    owners = lax.axis_size("ent")
    cap = max(2, 2 * edges // owners)
    slots = owners * cap
    share = -(-dim // owners)
    chunk = -(-(share + 1) // 16) * 16
    steps = owners.bit_length() - 1
    assert owners == 2**steps
    ent_t, rel_t = entity.T, relation.T
    as_row = lambda x: x.reshape(1, -1)
    src, rid = as_row(src_offset), as_row(rel_id)
    mac = lambda a, b, c: 2 * a * b * c
    dma = pltpu.SemaphoreType.DMA

    slot, asked, replies, sources, weights, queries = call(
        functools.partial(fetch_kernel, owners, cap),
        [
            ((1, edges), i32), ((owners, 8, cap), i32), ((owners, dim, cap), bf16),
            ((dim, edges), f32), ((dim, edges), f32), ((dim, edges), bf16),
        ],
        [
            VM((owners, 8, cap), i32), VM((owners, dim, cap), bf16),
            VM((3 * dim, rows), bf16), VM((3 * dim, nrel), bf16),
        ]
        + [dma((owners,))] * 4,
        flops=mac(3 * dim, rows + nrel, edges) + mac(dim, rows, slots),
        moved=dim * nrel * 8,
        collective_id=0,
        has_side_effects=True,
    )(as_row(dst_part), as_row(dst_offset), ent_t, rel_t, src, rid)
    edge_loss, coef, target_grad, targets = call(
        functools.partial(score_kernel, cap),
        [
            ((1, edges), f32), ((slots, edges), bf16),
            ((owners, dim + 16, cap), jnp.int16), ((dim, slots), bf16),
        ],
        [VM((slots, edges), f32)] + [VM((1, edges), f32)] * 3,
        flops=mac(2 * dim, slots, edges),
        moved=slots * edges * 2,
    )(queries, replies, slot)
    half = [VM((owners >> (k + 1), chunk, nrel), jnp.int16) for k in range(steps)]
    new_ent, ent_after, relation_code = call(
        functools.partial(return_kernel, owners, cap, share),
        [((dim, rows), f32), ((1, rows), f32), ((owners, chunk, nrel), jnp.int16)],
        [
            VM((owners, dim + 16, cap), jnp.int16), VM((2 * dim, edges), bf16),
            VM((2 * dim, edges), bf16), VM((owners, chunk, nrel), f32),
            VM((dim, rows), f32), VM((2 * dim, slots), bf16),
        ]
        + half + half + [dma((owners,))] * 2 + [dma((steps,))] * 4,
        flops=mac(dim, edges, slots + 2 * nrel + 2 * rows) + mac(2 * dim, slots, rows),
        moved=dim * nrel * 8,
        collective_id=1,
        has_side_effects=True,
    )(target_grad, targets, coef, sources, weights, src, rid, asked, ent_t, as_row(entity_state))
    new_rel, rel_after = call(
        functools.partial(relation_kernel, share),
        [((dim, nrel), f32), ((1, nrel), f32)],
        moved=dim * nrel * 10,
    )(relation_code, rel_t, as_row(relation_state))
    return (
        new_ent.T,
        ent_after.reshape(rows),
        new_rel.T,
        rel_after.reshape(nrel),
        edge_loss.reshape(edges),
    )


def solution(mesh):
    placed = (
        P(("groups", "ent"), None),
        P(("groups", "ent")),
        P("groups", None),
        P("groups"),
        P(("groups", "ent")),
        P(("groups", "ent"), None),
        P(("groups", "ent")),
        P(("groups", "ent")),
    )
    return jax.shard_map(
        on_device,
        mesh=mesh,
        in_specs=placed,
        out_specs=(
            P(("groups", "ent"), None),
            P(("groups", "ent")),
            P("groups", None),
            P("groups"),
            P(("groups", "ent")),
        ),
        check_vma=False,
    )
```

time: 207 us -> 165 us (0.80)
  waiting for transfers between devices: 17.4 us -> 0 us
  Pallas kernels: 146 us -> 161 us
  blocking collectives: 13.6 us -> 0 us
  starting transfers between devices: 13.4 us -> 0 us
  local copies, waits for them, and re-layouts: 14 us -> 2.37 us
    all_to_all x2 -> x0, waiting for transfers between devices: 17.4 us -> none  [the longest x1 17.4 us: on_device(): lax.all_to_all(looked, 'ent', split_axis=0, concat_axis=0, tiled=True)]
    all_to_all x1 -> x0, blocking collectives: 13.6 us -> none  [on_device(): lax.all_to_all(requests.reshape(owners, cap), 'ent', split_axis=0, concat...]
    all_to_all x2 -> x0, starting transfers between devices: 13.4 us -> none  [the longest x1 9.52 us: on_device(): lax.all_to_all(target_grad, 'ent', split_axis=0, concat_axis=0, tiled=True)]
    unnamed x38 -> x8, local copies, waits for them, and re-layouts: 14 us -> 1.77 us
    pallas_call x7 -> x3, Pallas kernels: 134 us -> 146 us  [the longest x1 87.2 us: on_device(): call(functools.partial(return_kernel, owners, cap, share), [((dim, rows),...]
    pallas_call x1, Pallas kernels: 12.4 us -> 14.6 us  [on_device(): call(functools.partial(score_kernel, cap), [((1, edges), f32), ((slots, e...]
  transfers between devices with their start and end apart: 2 -> 0, of which waited for: 1 -> 0; matrix products, arithmetic and copies ran while one was open for 0% -> 0% of each run, Pallas kernels for 58% -> 0%
where the time goes in v2:
time: 165 us
  Pallas kernels  161 us (98%)
  local copies, waits for them, and re-layouts  2.37 us (1%)
    pallas_call x1, Pallas kernels, on_device(): call(functools.partial(return_kernel, owners, cap, share), [((dim, rows),...  87.2 us
    pallas_call x1, Pallas kernels, on_device(): call(functools.partial(fetch_kernel, owners, cap), [((1, edges), i32), ((...  52.5 us
    pallas_call x1, Pallas kernels, on_device(): call(functools.partial(score_kernel, cap), [((1, edges), f32), ((slots, e...  14.6 us
    pallas_call x1, Pallas kernels, on_device(): call(functools.partial(relation_kernel, share), [((dim, nrel), f32), ((1,...  6.26 us

profile of v2, /device:TPU:0, one launch (start us, length us, event | category | flops | bytes accessed | tf_op | source)
XLA Modules:
  0.0 164.9 jit_solution(474548152721289831)
XLA Ops:
  0.6 52.5 %shard_map.119 = (s32[1,1024]{1,0:T(1,128)}, s32[16,8,128]{2,1,0:T(8,128)}, bf16[16,400,128]{2,1,0:T(8,128)(2,1)}, f32[400,1024]{1,0:T(8,128)}, f32[400,1024]{1,0:T(8,128)}, /*index=5*/bf16[400,1024]{1,0:T(8,128)(2,1)}) custom-call(s32[1,1024]{1,0:T(1,128)} %bitcast.18, s32[1,1024]{1,0:T(1,128)} %bitcast.19, f32[400,1024]{1,0:T(8,128)} %bitcast.16, ...), custom_call_target="tpu_custom_call" | custom-call | flops 9542041600 | bytes 6963200 | tf_op jit(solution)/shard_map/pallas_call | solution.py:405
  53.2 14.6 %shard_map.120 = (f32[1,1024]{1,0:T(1,128)}, bf16[2048,1024]{1,0:T(8,128)(2,1)}, s16[16,416,128]{2,1,0:T(8,128)(2,1)}, bf16[400,2048]{1,0:T(8,128)(2,1)}) custom-call(bf16[400,1024]{1,0:T(8,128)(2,1)} %get-tuple-element.20.q_ref, bf16[16,400,128]{2,1,0:T(8,128)(2,1)} %get-tuple-element.21.t_ref, s32[1,1024]{1,0:T(1,128)} %get-tuple-element.22.slot_ref), custom_call_target="tpu_custom_call" | custom-call | flops 3355443200 | bytes 4194304 | tf_op jit(solution)/shard_map/pallas_call | solution.py:421
  67.7 0.0 copy-start.1
  67.7 87.2 %shard_map.121 = (f32[400,1024]{1,0:T(8,128)}, f32[1,1024]{1,0:T(1,128)}, s16[16,32,2176]{2,1,0:T(8,128)(2,1)}) custom-call(s16[16,416,128]{2,1,0:T(8,128)(2,1)} %get-tuple-element.23.tg_ref, bf16[400,2048]{1,0:T(8,128)(2,1)} %get-tuple-element.24.tt_ref, bf16[2048,1024]{1,0:T(8,128)(2,1)} %get-tuple-element.25.c_ref, f32[400,1024]{1,0:T(8,128)} %get-tuple-element.26.s_ref, ...), custom_call_target="tpu_custom_call" | custom-call | flops 10276044800 | bytes 6963200 | tf_op jit(solution)/shard_map/pallas_call | solution.py:432
  155.0 0.0 copy-done.1
  155.0 0.6 reshape.43.state_ref
  155.6 0.0 copy-start
  155.6 6.3 %shard_map.122 = (f32[400,2176]{1,0:T(8,128)}, f32[1,2176]{1,0:T(1,128)}) custom-call(s16[16,32,2176]{2,1,0:T(8,128)(2,1)} %get-tuple-element.31.code_ref, f32[400,2176]{1,0:T(8,128)} %bitcast.12, f32[1,2176]{1,0:T(1,128)} %reshape.43.state_ref), custom_call_target="tpu_custom_call" | custom-call | bytes 8704000 | tf_op jit(solution)/shard_map/pallas_call | solution.py:446
  161.8 1.3 reduce
  163.2 0.0 copy-done
  163.2 0.0 copy-start.2
  163.2 1.2 copy.15
  164.3 0.0 copy-done.2
  164.3 0.6 copy.16
Async XLA Ops:
  67.7 87.2 %copy-start.1 = (f32[2176]{0:T(1024)S(1)}, f32[2176]{0:T(1024)}, u32[]{:S(2)}) copy-start(f32[2176]{0:T(1024)} %param.11) | copy-start | bytes 26116
  155.6 7.6 %copy-start = (f32[400,1024]{1,0:T(8,128)S(1)}, f32[400,1024]{1,0:T(8,128)}, u32[]{:S(2)}) copy-start(f32[400,1024]{1,0:T(8,128)} %get-tuple-element.29) | copy-start | bytes 4915204
  163.2 1.2 copy-start.2

commit v3 on v2

--- a/solution.py
+++ b/solution.py
@@ -85,9 +85,9 @@
     return copy
 
 
-def each_peer(owners, body):
+def each_peer(owners, body, first=1):
     def step(t, carry):
-        body(1 + (owners // 2 - 1 + t) % (owners - 1))
+        body(1 + (first - 1 + t) % (owners - 1))
         return carry
 
     lax.fori_loop(0, owners - 1, step, 0)
@@ -233,22 +233,26 @@
 
 
 def return_kernel(
-    owners, cap, share, tg_ref, tt_ref, c_ref, s_ref, w_ref, src_ref, rid_ref, asked_ref,
-    ent_ref, state_ref, new_ref, after_ref, out_ref,
-    arrived, high2, terms2, acc, part, both, *rest,
+    owners, cap, share, pieces, tg_ref, tt_ref, c_ref, s_ref, w_ref, src_ref, rid_ref, asked_ref,
+    ent_ref, state_ref, new_ref, after_ref, *rest,
 ):
     steps = owners.bit_length() - 1
-    boxes, bags = rest[:steps], rest[steps : 2 * steps]
-    send0, recv0, send1, recv1, send2, recv2 = rest[2 * steps :]
+    count = len(pieces)
+    outs, rest = rest[:count], rest[count:]
+    arrived, high2, terms2, part, both, send0, recv0, send1, recv1, send2, recv2 = rest[:11]
+    accs, rest = rest[11 : 11 + count], rest[11 + count :]
+    boxes = [rest[p * steps : (p + 1) * steps] for p in range(count)]
+    rest = rest[count * steps :]
+    bags = [rest[p * steps : (p + 1) * steps] for p in range(count)]
     me = lax.axis_index("ent")
     barrier = greet(owners, me)
     pl.semaphore_wait(barrier, owners - 1)
     grads_out = swap(owners, me, tg_ref, arrived, send0, recv0)
-    each_peer(owners, lambda d: grads_out(d).start())
+    each_peer(owners, lambda d: grads_out(d).start(), owners // 2)
     arrived[me] = tg_ref[me]
 
     dim, edges = s_ref.shape
-    chunk = acc.shape[1]
+    chunk = accs[0].shape[1]
 
     def halves(into, at, x):
         high = x.astype(bf16)
@@ -263,19 +267,18 @@
 
     tiles(edges, grads)
 
-    def relation(start, width):
+    def relation(p, start, width):
+        acc = accs[p]
         at = pl.ds(start, width)
-        got = nt(terms2[...], ones_at(start, width, rid_ref[...]))
+        got = nt(terms2[...], ones_at(pieces[p][0] + start, width, rid_ref[...]))
         got = got[0:dim] + got[dim:]
         for c in range(owners):
             low, high = min(c * share, dim), min((c + 1) * share, dim)
             gap = jnp.zeros((chunk - (high - low), width), f32)
             acc[c, :, at] = jnp.concatenate([got[low:high], gap], axis=0) if high > low else gap
 
-    tiles(acc.shape[2], relation)
-
-    def pack(c):
-        code, power = encode(acc[c])
+    def pack(p, c):
+        code, power = encode(accs[p][c])
         last = lax.broadcasted_iota(i32, code.shape, 0) == chunk - 1
         return short(jnp.where(last, power, code))
 
@@ -313,41 +316,67 @@
 
     bit = [(me // 2**k) % 2 for k in range(steps)]
     mate = [me + (1 - 2 * bit[k]) * 2**k for k in range(steps)]
-    low, size, lows = 0, owners, []
-    for k in range(steps):
-        lows.append((low, size))
+    place = [(0, owners)] * count
+    past = [[] for _ in pieces]
+    flying = [None] * count
+
+    def give(p, k):
+        b = pieces[p][2][k]
+        low, size = place[p]
         half = size // 2
-        keep, give = low + bit[k] * half, low + (1 - bit[k]) * half
+        past[p].append((low, size))
+        away = low + (1 - bit[b]) * half
 
         def fill(c, carry):
-            bags[k][c] = pack(give + c)
+            bags[p][k][c] = pack(p, away + c)
             return carry
 
         lax.fori_loop(0, half, fill, 0)
-        copy = remote(bags[k], boxes[k], mate[k], send1.at[k], recv1.at[k])
-        copy.start()
-        if k == 0:
-            tiles(ent_ref.shape[1], entity_part)
-        copy.wait()
+        at = p * steps + k
+        flying[p] = remote(bags[p][k], boxes[p][k], mate[b], send1.at[at], recv1.at[at])
+        flying[p].start()
+        place[p] = (low + bit[b] * half, half)
+
+    def take(p, k):
+        flying[p].wait()
+        low, half = place[p]
 
         def add(c, carry):
-            got = wide(boxes[k][c])
+            got = wide(boxes[p][k][c])
             body = got * quantum(got[chunk - 1 :])
             last = lax.broadcasted_iota(i32, got.shape, 0) == chunk - 1
-            acc[keep + c] = acc[keep + c] + jnp.where(last, 0.0, body)
+            accs[p][low + c] = accs[p][low + c] + jnp.where(last, 0.0, body)
             return carry
 
         lax.fori_loop(0, half, add, 0)
-        low, size = keep, half
-    out_ref[low] = pack(low)
+
+    def share_out(p, k):
+        b = pieces[p][2][k]
+        low, size = past[p][k]
+        here = outs[p].at[pl.ds(low + bit[b] * (size // 2), size // 2)]
+        at = p * steps + k
+        flying[p] = remote(here, here, mate[b], send2.at[at], recv2.at[at])
+        flying[p].start()
+
+    for p in range(count):
+        tiles(pieces[p][1], functools.partial(relation, p))
+        give(p, 0)
+    tiles(ent_ref.shape[1], entity_part)
+    for k in range(steps):
+        for p in range(count):
+            take(p, k)
+            if k < steps - 1:
+                give(p, k + 1)
+            else:
+                outs[p][place[p][0]] = pack(p, place[p][0])
+                share_out(p, k)
     for k in reversed(range(steps)):
-        half = lows[k][1] // 2
-        place = out_ref.at[pl.ds(lows[k][0] + bit[k] * half, half)]
-        copy = remote(place, place, mate[k], send2.at[k], recv2.at[k])
-        copy.start()
         if k == min(1, steps - 1):
             entity_all()
-        copy.wait()
+        for p in range(count):
+            flying[p].wait()
+            if k:
+                share_out(p, k - 1)
 
 
 def step_rows(value, state, grad):
@@ -355,20 +384,23 @@
     return value - grad * (learn_rate / jnp.sqrt(after)), after
 
 
-def relation_kernel(share, code_ref, rel_ref, state_ref, new_ref, after_ref):
+def relation_kernel(share, pieces, *refs):
+    codes, (rel_ref, state_ref, new_ref, after_ref) = refs[:-4], refs[-4:]
     dim = rel_ref.shape[0]
-
-    def body(start, width):
-        at = pl.ds(start, width)
-        pieces = []
+    chunk = codes[0].shape[1]
+
+    def body(p, start, width):
+        found = []
         for c in range(-(-dim // share)):
-            got = wide(code_ref[c, :, at])
+            got = wide(codes[p][c, :, pl.ds(start, width)])
             used = min(share, dim - c * share)
-            pieces.append(got[0:used] * quantum(got[code_ref.shape[1] - 1 :]))
-        grad = jnp.concatenate(pieces, axis=0)
+            found.append(got[0:used] * quantum(got[chunk - 1 :]))
+        grad = jnp.concatenate(found, axis=0)
+        at = pl.ds(pieces[p][0] + start, width)
         new_ref[:, at], after_ref[:, at] = step_rows(rel_ref[:, at], state_ref[:, at], grad)
 
-    tiles(rel_ref.shape[1], body)
+    for p in range(len(pieces)):
+        tiles(pieces[p][1], functools.partial(body, p))
 
 
 def call(kernel, outs, scratch=(), flops=0, moved=0, **extra):
@@ -428,26 +460,36 @@
         flops=mac(2 * dim, slots, edges),
         moved=slots * edges * 2,
     )(queries, replies, slot)
-    half = [VM((owners >> (k + 1), chunk, nrel), jnp.int16) for k in range(steps)]
-    new_ent, ent_after, relation_code = call(
-        functools.partial(return_kernel, owners, cap, share),
-        [((dim, rows), f32), ((1, rows), f32), ((owners, chunk, nrel), jnp.int16)],
+    first = -(-nrel // 256) * 128
+    order = list(range(steps))
+    other = order[:1] + order[2:] + order[1:2]
+    pieces = [(0, first, order), (first, nrel - first, other)]
+    half = [
+        VM((owners >> (k + 1), chunk, wide_), jnp.int16) for _, wide_, _ in pieces for k in range(steps)
+    ]
+    new_ent, ent_after, *codes = call(
+        functools.partial(return_kernel, owners, cap, share, pieces),
+        [((dim, rows), f32), ((1, rows), f32)]
+        + [((owners, chunk, wide_), jnp.int16) for _, wide_, _ in pieces],
         [
             VM((owners, dim + 16, cap), jnp.int16), VM((2 * dim, edges), bf16),
-            VM((2 * dim, edges), bf16), VM((owners, chunk, nrel), f32),
-            VM((dim, rows), f32), VM((2 * dim, slots), bf16),
+            VM((2 * dim, edges), bf16), VM((dim, rows), f32), VM((2 * dim, slots), bf16),
         ]
-        + half + half + [dma((owners,))] * 2 + [dma((steps,))] * 4,
+        + [dma((owners,))] * 2
+        + [dma((len(pieces) * steps,))] * 4
+        + [VM((owners, chunk, wide_), f32) for _, wide_, _ in pieces]
+        + half
+        + half,
         flops=mac(dim, edges, slots + 2 * nrel + 2 * rows) + mac(2 * dim, slots, rows),
         moved=dim * nrel * 8,
         collective_id=1,
         has_side_effects=True,
     )(target_grad, targets, coef, sources, weights, src, rid, asked, ent_t, as_row(entity_state))
     new_rel, rel_after = call(
-        functools.partial(relation_kernel, share),
+        functools.partial(relation_kernel, share, pieces),
         [((dim, nrel), f32), ((1, nrel), f32)],
         moved=dim * nrel * 10,
-    )(relation_code, rel_t, as_row(relation_state))
+    )(*codes, rel_t, as_row(relation_state))
     return (
         new_ent.T,
         ent_after.reshape(rows),

time: 165 us -> 156 us (0.945)
  Pallas kernels: 161 us -> 152 us
    pallas_call x1, Pallas kernels: 52.5 us -> 43.9 us  [on_device(): call(functools.partial(fetch_kernel, owners, cap), [((1, edges), i32), ((...]
where the time goes in v3:
time: 156 us
  Pallas kernels  152 us (97%)
  local copies, waits for them, and re-layouts  2.37 us (2%)
    pallas_call x1, Pallas kernels, on_device(): call(functools.partial(return_kernel, owners, cap, share, pieces), [((dim...  87 us
    pallas_call x1, Pallas kernels, on_device(): call(functools.partial(fetch_kernel, owners, cap), [((1, edges), i32), ((...  43.9 us
    pallas_call x1, Pallas kernels, on_device(): call(functools.partial(score_kernel, cap), [((1, edges), f32), ((slots, e...  14.6 us
    pallas_call x1, Pallas kernels, on_device(): call(functools.partial(relation_kernel, share, pieces), [((dim, nrel), f3...  6.24 us

profile of v3, /device:TPU:0, one launch (start us, length us, event | category | flops | bytes accessed | tf_op | source)
XLA Modules:
  0.0 156.1 jit_solution(13617356872438853062)
XLA Ops:
  0.6 43.9 %shard_map.119 = (s32[1,1024]{1,0:T(1,128)}, s32[16,8,128]{2,1,0:T(8,128)}, bf16[16,400,128]{2,1,0:T(8,128)(2,1)}, f32[400,1024]{1,0:T(8,128)}, f32[400,1024]{1,0:T(8,128)}, /*index=5*/bf16[400,1024]{1,0:T(8,128)(2,1)}) custom-call(s32[1,1024]{1,0:T(1,128)} %bitcast.18, s32[1,1024]{1,0:T(1,128)} %bitcast.19, f32[400,1024]{1,0:T(8,128)} %bitcast.16, ...), custom_call_target="tpu_custom_call" | custom-call | flops 9542041600 | bytes 6963200 | tf_op jit(solution)/shard_map/pallas_call | solution.py:437
  44.5 14.6 %shard_map.120 = (f32[1,1024]{1,0:T(1,128)}, bf16[2048,1024]{1,0:T(8,128)(2,1)}, s16[16,416,128]{2,1,0:T(8,128)(2,1)}, bf16[400,2048]{1,0:T(8,128)(2,1)}) custom-call(bf16[400,1024]{1,0:T(8,128)(2,1)} %get-tuple-element.21.q_ref, bf16[16,400,128]{2,1,0:T(8,128)(2,1)} %get-tuple-element.22.t_ref, s32[1,1024]{1,0:T(1,128)} %get-tuple-element.23.slot_ref), custom_call_target="tpu_custom_call" | custom-call | flops 3355443200 | bytes 4194304 | tf_op jit(solution)/shard_map/pallas_call | solution.py:453
  59.1 0.0 copy-start.1
  59.1 87.0 %shard_map.121 = (f32[400,1024]{1,0:T(8,128)}, f32[1,1024]{1,0:T(1,128)}, s16[16,32,1152]{2,1,0:T(8,128)(2,1)}, s16[16,32,1024]{2,1,0:T(8,128)(2,1)}) custom-call(s16[16,416,128]{2,1,0:T(8,128)(2,1)} %get-tuple-element.24.tg_ref, bf16[400,2048]{1,0:T(8,128)(2,1)} %get-tuple-element.25.tt_ref, bf16[2048,1024]{1,0:T(8,128)(2,1)} %get-tuple-element.26.c_ref, ...), custom_call_target="tpu_custom_call" | custom-call | flops 10276044800 | bytes 6963200 | tf_op jit(solution)/shard_map/pallas_call | solution.py:470
  146.1 0.0 copy-done.1
  146.1 0.6 reshape.43.refs_3_
  146.7 0.0 copy-start
  146.7 6.2 %shard_map.122 = (f32[400,2176]{1,0:T(8,128)}, f32[1,2176]{1,0:T(1,128)}) custom-call(s16[16,32,1152]{2,1,0:T(8,128)(2,1)} %get-tuple-element.32.refs_0_, s16[16,32,1024]{2,1,0:T(8,128)(2,1)} %get-tuple-element.33.refs_1_, f32[400,2176]{1,0:T(8,128)} %bitcast.12, f32[1,2176]{1,0:T(1,128)} %reshape.43.refs_3_), custom_call_target="tpu_custom_call" | custom-call | bytes 8704000 | tf_op jit(solution)/shard_map/pallas_call | solution.py:488
  153.0 1.3 reduce
  154.3 0.0 copy-done
  154.3 0.0 copy-start.2
  154.3 1.2 copy.15
  155.5 0.0 copy-done.2
  155.5 0.6 copy.16
Async XLA Ops:
  59.1 87.0 %copy-start.1 = (f32[2176]{0:T(1024)S(1)}, f32[2176]{0:T(1024)}, u32[]{:S(2)}) copy-start(f32[2176]{0:T(1024)} %param.11) | copy-start | bytes 26116
  146.7 7.6 %copy-start = (f32[400,1024]{1,0:T(8,128)S(1)}, f32[400,1024]{1,0:T(8,128)}, u32[]{:S(2)}) copy-start(f32[400,1024]{1,0:T(8,128)} %get-tuple-element.30) | copy-start | bytes 4915204
  154.3 1.2 copy-start.2
